TPU v7x, 32 devices: a whole 2x2x4 slice. The times are simulated.
32 devices in a mesh: cases: 2 (over y), tm: 4 (over z), region: 4 (over x, core).
Axes of the slice: x: 2, y: 2, z: 4, core: 2. Of those that a mesh axis runs over, the one named last changes fastest.
Arguments:
- former_estimate: float32 [384, 32, 128], P(('cases', 'tm'), 'region'), parts along dimension 0, may hold values from -6 to 6
- excitation: bfloat16 [384, 32, 128], P(('cases', 'tm'), 'region'), parts along dimension 0, may hold values from -6 to 6
- susceptance_maps: bfloat16 [32, 4, 128, 128], P('region'), may hold values from -0.125 to 0.125
- linked_partner_target: int32 [32, 4], P('region'), may hold values from 0 to 31, as said below
- attenuation: float32 [32, 64], P('region'), may hold values from 0.0002 to 0.03
- revolution_angle: float32 [32, 64], P('region'), may hold values from -0.6 to 0.6
- saturated_flag: int32 [64, 64], P(('cases', 'region')), parts along dimension 0, may hold values 0 or 1
- gain_surge: float32 [384], P(('cases', 'tm')), parts along dimension 0, may hold values from 0.25 to 1
Outputs:
- waveform: float32 [384, 32, 128], P(('cases', 'tm'), 'region'), parts along dimension 0
There are 2 independent parts, one for each index of `cases`. A program takes and returns all parts, laid end to end along the dimension named above; an argument that names none is the same for every part. Nothing has to cross between parts.
Inputs may be any that keep to these rules, and one draw needn't show every extreme that they name: `linked_partner_target`: block row b lies in region g = b // 8. Its column 0 is b itself, column 1 a block of region g, column 2 one of the last 4 blocks of region g - 1 and column 3 one of the first 4 blocks of region g + 1, regions counted around a cycle of 32 // 8.
All inputs are finite; a program needn't handle non-finite values. No bound on the sum of `saturated_flag` on one device may be relied on, other than what follows from the above.
Results may differ from a plain program's by a relative error of at most 0.0017.
Values may be sent and summed in bfloat16 or wider, within the bound.
A program may use at most 64 MiB of HBM per device.

v0:
```python
import jax
import jax.numpy as jnp
from jax import lax
from jax.sharding import PartitionSpec as P

BND = 4
SWEEPS = 3


clip_level = 0.5


def with_halo(block, sides, width):
    for axis, dim in sides:
        count = lax.axis_size(axis)
        forward = [(i, i + 1) for i in range(count - 1)]
        forward.append((count - 1, 0))
        backward = [(target, source) for source, target in forward]
        low = lax.ppermute(
            lax.slice_in_dim(block, block.shape[dim] - width, None, axis=dim), axis, forward
        )
        high = lax.ppermute(lax.slice_in_dim(block, 0, width, axis=dim), axis, backward)
        block = jnp.concatenate([low, block, high], axis=dim)
    return block


def complex_mul(first, second):
    half = first.shape[-1] // 2
    first_re, first_im = (first[..., :half], first[..., half:])
    second_re, second_im = (second[..., :half], second[..., half:])
    return jnp.concatenate(
        [first_re * second_re - first_im * second_im, first_re * second_im + first_im * second_re],
        axis=-1,
    )


def combine(early, late):
    return (complex_mul(late[0], early[0]), complex_mul(late[0], early[1]) + late[1])


def bus_terms(attenuation, revolution_angle):
    modulus = jnp.exp(-attenuation)
    cosine = modulus * jnp.cos(revolution_angle)
    sine = modulus * jnp.sin(revolution_angle)
    argument_spin = jnp.concatenate([cosine, sine], axis=-1)
    input_gain = jnp.sqrt((1.0 - cosine) ** 2 + sine**2)
    return (argument_spin, jnp.concatenate([input_gain, input_gain], axis=-1))


def limit_current(current, saturated_flag):
    half = current.shape[-1] // 2
    square = current[..., :half] ** 2 + current[..., half:] ** 2
    scaling_factor = jnp.where(
        saturated_flag == 1, clip_level / jnp.sqrt(clip_level**2 + square), 1.0
    )
    return current * jnp.concatenate([scaling_factor, scaling_factor], axis=-1)


def periodic_end(total_a, total_b):
    half = total_a.shape[-1] // 2
    denom_re = 1.0 - total_a[..., :half]
    denom_im = -total_a[..., half:]
    square = denom_re**2 + denom_im**2
    conjugate = jnp.concatenate([denom_re / square, -denom_im / square], axis=-1)
    return complex_mul(total_b, conjugate)


def local(
    former_estimate,
    excitation,
    susceptance_maps,
    linked_partner_target,
    attenuation,
    revolution_angle,
    saturated_flag,
    gain_surge,
):
    blocks = former_estimate.shape[1]
    buses = attenuation.shape[1]
    argument_spin, input_gain = bus_terms(attenuation, revolution_angle)
    incremental_spin = gain_surge[:, None, None] * argument_spin[None]
    drive_base = excitation.astype(jnp.float32)
    region_index = lax.axis_index("region")
    network = blocks * lax.axis_size("region")
    local_col = (linked_partner_target - region_index * blocks) % network
    local_col = jnp.where(local_col >= network - BND, local_col - network, local_col) + BND
    unit = jnp.concatenate(
        [jnp.ones((blocks, buses), jnp.float32), jnp.zeros((blocks, buses), jnp.float32)], axis=-1
    )
    nothing = jnp.zeros((blocks, 2 * buses), jnp.float32)
    wave = former_estimate
    for sweep_index in range(SWEEPS):
        rounded = wave.astype(jnp.bfloat16)
        extended = with_halo(rounded, (("region", 1),), BND)
        picked = extended[:, local_col, :]
        current = jnp.einsum(
            "tbkj,bkij->tbi", picked, susceptance_maps, preferred_element_type=jnp.float32
        )
        drive = input_gain[None] * (drive_base - limit_current(current, saturated_flag[None]))
        local_a, local_b = lax.associative_scan(combine, (incremental_spin, drive), axis=0)
        own_map = (local_a[-1], local_b[-1])
        every_a, every_b = (
            lax.all_gather(own_map[0][None], "tm", axis=0, tiled=True),
            lax.all_gather(own_map[1][None], "tm", axis=0, tiled=True),
        )
        run_a, run_b = lax.associative_scan(combine, (every_a, every_b), axis=0)
        total_a, total_b = (run_a[-1], run_b[-1])
        time_index = lax.axis_index("tm")
        earlier = jnp.maximum(time_index - 1, 0)
        prior_a = lax.dynamic_index_in_dim(run_a, earlier, 0, keepdims=False)
        prior_b = lax.dynamic_index_in_dim(run_b, earlier, 0, keepdims=False)
        before = (
            jnp.where(time_index > 0, prior_a, unit),
            jnp.where(time_index > 0, prior_b, nothing),
        )
        end_state = periodic_end(total_a, total_b)
        start_state = complex_mul(before[0], end_state) + before[1]
        wave = complex_mul(local_a, start_state[None]) + local_b
    return wave


def solution(mesh):
    in_specs = (
        P(("cases", "tm"), "region", None),
        P(("cases", "tm"), "region", None),
        P("region", None, None, None),
        P("region", None),
        P("region", None),
        P("region", None),
        P(("cases", "region"), None),
        P(("cases", "tm")),
    )
    out_specs = P(("cases", "tm"), "region", None)
    return jax.shard_map(local, mesh=mesh, in_specs=in_specs, out_specs=out_specs, check_vma=False)
```

profile of v0, /device:TPU:0, one launch (start us, length us, event | category | flops | bytes accessed | tf_op | source)
XLA Modules:
  0.0 90.0 jit_solution(5454847663768018754)
XLA Ops:
  0.0 1.1 %copy.114 = bf16[48,8,128]{2,0,1:T(8,128)(2,1)S(1)} copy(f32[48,8,128]{2,1,0:T(8,128)} %param.8) | data formatting | bytes 294912 | tf_op args[0]
  1.1 0.5 collective-permute-start
  1.6 2.0 %collective-permute-start.1 = (bf16[48,4,128]{2,0,1:T(8,128)(2,1)S(1)}, bf16[48,4,128]{2,0,1:T(8,128)(2,1)S(1)}, u32[]{:S(2)}, u32[]{:S(2)}) collective-permute-start(bf16[48,4,128]{2,0,1:T(8,128)(2,1)S(1)} %get-tuple-element.68), channel_id=1, source_target_pairs={{1,0},{2,1},{3,2},{0,3},{5,4},{6,5},{7,6},{4,7},{9,8},{10,9},{11,1... | collective-permute-start | bytes 147464 | tf_op jit(solution)/shard_map/ppermute | solution.py:22
  3.6 0.7 copy-done.9
  4.5 0.5 copy-done.5
  5.1 0.7 copy-done.10
  5.9 0.6 copy-done.1
  6.6 0.6 gather_fusion
  8.0 0.7 copy-done.2
  12.4 0.5 slice-done
  13.4 14.1 %all_gather.14 = f32[4,8,128]{2,1,0:T(8,128)S(1)} all-gather(f32[1,8,128]{2,1,0:T(8,128)S(1)} %slice_add_fusion.40), channel_id=1, replica_groups=mesh['cases'=2,'tm'=4,'region'=4] {'tm'}, dimensions={0}, use_global_device_ids=true | all-gather | bytes 20480 | tf_op jit(solution)/shard_map/all_gather | solution.py:103
  28.5 13.1 %all_gather.15 = f32[4,8,128]{2,1,0:T(8,128)S(1)} all-gather(f32[1,8,128]{2,1,0:T(8,128)S(1)} %slice_add_fusion.37), channel_id=1, replica_groups=mesh['cases'=2,'tm'=4,'region'=4] {'tm'}, dimensions={0}, use_global_device_ids=true | all-gather | bytes 20480 | tf_op jit(solution)/shard_map/all_gather | solution.py:104
  42.3 0.7 slice-done.1
  43.0 0.7 copy-done.7
  44.5 1.7 %collective-permute-start.3 = (bf16[48,4,128]{2,1,0:T(4,128)(2,1)S(1)}, bf16[48,4,128]{2,1,0:T(4,128)(2,1)S(1)}, u32[]{:S(2)}, u32[]{:S(2)}) collective-permute-start(bf16[48,4,128]{2,1,0:T(4,128)(2,1)S(1)} %get-tuple-element.62), channel_id=1, source_target_pairs={{1,0},{2,1},{3,2},{0,3},{5,4},{6,5},{7,6},{4,7},{9,8},{10,9},{11,1... | collective-permute-start | bytes 147464 | tf_op jit(solution)/shard_map/ppermute | solution.py:22
  46.2 1.8 %collective-permute-done.2 = bf16[48,4,128]{2,1,0:T(4,128)(2,1)S(1)} collective-permute-done((bf16[48,4,128]{2,1,0:T(4,128)(2,1)S(1)}, bf16[48,4,128]{2,1,0:T(4,128)(2,1)S(1)}, u32[]{:S(2)}, u32[]{:S(2)}) %collective-permute-start.2) | collective-permute-done | bytes 49184 | tf_op jit(solution)/shard_map/ppermute | solution.py:19
  48.2 0.6 gather_fusion.1
  52.4 13.1 %all_gather.16 = f32[4,8,128]{2,1,0:T(8,128)S(1)} all-gather(f32[1,8,128]{2,1,0:T(8,128)S(1)} %slice_add_fusion.32), channel_id=1, replica_groups=mesh['cases'=2,'tm'=4,'region'=4] {'tm'}, dimensions={0}, use_global_device_ids=true | all-gather | bytes 20480 | tf_op jit(solution)/shard_map/all_gather | solution.py:104
  65.8 0.6 copy-done.4
  67.3 1.7 %collective-permute-start.5 = (bf16[48,4,128]{2,1,0:T(4,128)(2,1)S(1)}, bf16[48,4,128]{2,1,0:T(4,128)(2,1)S(1)}, u32[]{:S(2)}, u32[]{:S(2)}) collective-permute-start(bf16[48,4,128]{2,1,0:T(4,128)(2,1)S(1)} %get-tuple-element.58), channel_id=1, source_target_pairs={{1,0},{2,1},{3,2},{0,3},{5,4},{6,5},{7,6},{4,7},{9,8},{10,9},{11,1... | collective-permute-start | bytes 147464 | tf_op jit(solution)/shard_map/ppermute | solution.py:22
  69.0 1.8 %collective-permute-done.4 = bf16[48,4,128]{2,1,0:T(4,128)(2,1)S(1)} collective-permute-done((bf16[48,4,128]{2,1,0:T(4,128)(2,1)S(1)}, bf16[48,4,128]{2,1,0:T(4,128)(2,1)S(1)}, u32[]{:S(2)}, u32[]{:S(2)}) %collective-permute-start.4) | collective-permute-done | bytes 49184 | tf_op jit(solution)/shard_map/ppermute | solution.py:19
  70.9 0.6 gather_fusion.2
  75.2 13.1 %all_gather.17 = f32[4,8,128]{2,1,0:T(8,128)S(1)} all-gather(f32[1,8,128]{2,1,0:T(8,128)S(1)} %slice_add_fusion.27), channel_id=1, replica_groups=mesh['cases'=2,'tm'=4,'region'=4] {'tm'}, dimensions={0}, use_global_device_ids=true | all-gather | bytes 20480 | tf_op jit(solution)/shard_map/all_gather | solution.py:104
  89.2 0.8 maximum_add_fusion.2
  (290 shorter events, 16.2 us)
Async XLA Ops:
  0.0 7.3 %copy-start = (bf16[8,4,128,128]{3,2,1,0:T(8,128)(2,1)S(1)}, bf16[8,4,128,128]{3,2,1,0:T(8,128)(2,1)}, u32[]{:S(2)}) copy-start(bf16[8,4,128,128]{3,2,1,0:T(8,128)(2,1)} %param.10) | copy-start | bytes 3145732
  1.1 2.5 %copy-start.8 = (s32[8,64]{1,0:T(8,128)S(1)}, s32[8,64]{1,0:T(8,128)}, u32[]{:S(2)}) copy-start(s32[8,64]{1,0:T(8,128)} %param.14) | copy-start | bytes 6148
  1.1 5.5 %collective-permute-start = (bf16[48,4,128]{2,0,1:T(8,128)(2,1)S(1)}, bf16[48,4,128]{2,0,1:T(8,128)(2,1)S(1)}, u32[]{:S(2)}, u32[]{:S(2)}) collective-permute-start(bf16[48,4,128]{2,0,1:T(8,128)(2,1)S(1)} %get-tuple-element.67), channel_id=1, source_target_pairs={{0,1},{1,2},{2,3},{3,0},{4,5},{5,6},{6,7},{7,4},{8,9},{9,10},{10,1... | collective-permute-start | bytes 147464 | tf_op jit(solution)/shard_map/ppermute | solution.py:19
  1.6 5.0 %collective-permute-start.1 = (bf16[48,4,128]{2,0,1:T(8,128)(2,1)S(1)}, bf16[48,4,128]{2,0,1:T(8,128)(2,1)S(1)}, u32[]{:S(2)}, u32[]{:S(2)}) collective-permute-start(bf16[48,4,128]{2,0,1:T(8,128)(2,1)S(1)} %get-tuple-element.68), channel_id=1, source_target_pairs={{1,0},{2,1},{3,2},{0,3},{5,4},{6,5},{7,6},{4,7},{9,8},{10,9},{11,1... | collective-permute-start | bytes 147464 | tf_op jit(solution)/shard_map/ppermute | solution.py:22
  3.6 0.7 copy-start.9
  4.3 0.7 copy-start.5
  4.3 0.7 copy-start.6
  5.1 0.7 copy-start.10
  5.9 0.7 copy-start.1
  7.8 0.9 copy-start.2
  12.2 0.7 slice-start
  27.5 14.5 %copy-start.3 = (f32[4,8,128]{2,1,0:T(8,128)}, f32[4,8,128]{2,1,0:T(8,128)S(1)}, u32[]{:S(2)}) copy-start(f32[4,8,128]{2,1,0:T(8,128)S(1)} %all_gather.14) | copy-start | bytes 49156
  42.3 0.7 slice-start.1
  43.0 0.7 copy-start.7
  44.4 3.6 %collective-permute-start.2 = (bf16[48,4,128]{2,1,0:T(4,128)(2,1)S(1)}, bf16[48,4,128]{2,1,0:T(4,128)(2,1)S(1)}, u32[]{:S(2)}, u32[]{:S(2)}) collective-permute-start(bf16[48,4,128]{2,1,0:T(4,128)(2,1)S(1)} %get-tuple-element.61), channel_id=1, source_target_pairs={{0,1},{1,2},{2,3},{3,0},{4,5},{5,6},{6,7},{7,4},{8,9},{9,10},{10,1... | collective-permute-start | bytes 147464 | tf_op jit(solution)/shard_map/ppermute | solution.py:19
  44.5 3.5 %collective-permute-start.3 = (bf16[48,4,128]{2,1,0:T(4,128)(2,1)S(1)}, bf16[48,4,128]{2,1,0:T(4,128)(2,1)S(1)}, u32[]{:S(2)}, u32[]{:S(2)}) collective-permute-start(bf16[48,4,128]{2,1,0:T(4,128)(2,1)S(1)} %get-tuple-element.62), channel_id=1, source_target_pairs={{1,0},{2,1},{3,2},{0,3},{5,4},{6,5},{7,6},{4,7},{9,8},{10,9},{11,1... | collective-permute-start | bytes 147464 | tf_op jit(solution)/shard_map/ppermute | solution.py:22
  65.7 0.7 copy-start.4
  67.2 3.6 %collective-permute-start.4 = (bf16[48,4,128]{2,1,0:T(4,128)(2,1)S(1)}, bf16[48,4,128]{2,1,0:T(4,128)(2,1)S(1)}, u32[]{:S(2)}, u32[]{:S(2)}) collective-permute-start(bf16[48,4,128]{2,1,0:T(4,128)(2,1)S(1)} %get-tuple-element.57), channel_id=1, source_target_pairs={{0,1},{1,2},{2,3},{3,0},{4,5},{5,6},{6,7},{7,4},{8,9},{9,10},{10,1... | collective-permute-start | bytes 147464 | tf_op jit(solution)/shard_map/ppermute | solution.py:19
  67.3 3.5 %collective-permute-start.5 = (bf16[48,4,128]{2,1,0:T(4,128)(2,1)S(1)}, bf16[48,4,128]{2,1,0:T(4,128)(2,1)S(1)}, u32[]{:S(2)}, u32[]{:S(2)}) collective-permute-start(bf16[48,4,128]{2,1,0:T(4,128)(2,1)S(1)} %get-tuple-element.58), channel_id=1, source_target_pairs={{1,0},{2,1},{3,2},{0,3},{5,4},{6,5},{7,6},{4,7},{9,8},{10,9},{11,1... | collective-permute-start | bytes 147464 | tf_op jit(solution)/shard_map/ppermute | solution.py:22
where the time goes:
time: 90.4 us; the launch traced here: 90 us
  blocking collectives  53.5 us (59%)
  local copies, waits for them, and re-layouts  12.5 us (14%)
  other arithmetic  11.7 us (13%)
  starting transfers between devices  6.07 us (7%)
  waiting for transfers between devices  3.55 us (4%)
  matrix products  1.36 us (2%)
  between operations  1.28 us (1%)
    all_gather x3, blocking collectives, local(): lax.all_gather(own_map[1][None], 'tm', axis=0, tiled=True)  39.4 us
    all_gather x1, blocking collectives, local(): lax.all_gather(own_map[0][None], 'tm', axis=0, tiled=True)  14.1 us
    unnamed x26, local copies, waits for them, and re-layouts  5.99 us
    ppermute x3, starting transfers between devices, with_halo(): lax.ppermute(lax.slice_in_dim(block, 0, width, axis=dim), axis, backward)  5.45 us
    sub x45, other arithmetic, complex_mul(): first_re * second_re - first_im * second_im  4.13 us
    ppermute x3, waiting for transfers between devices, with_halo(): lax.ppermute(lax.slice_in_dim(block, block.shape[dim] - width, None, axis...  3.54 us
    add x33, other arithmetic, combine(): complex_mul(late[0], early[1]) + late[1]  2.7 us
    pad x34, local copies, waits for them, and re-layouts, local(): lax.associative_scan(combine, (incremental_spin, drive), axis=0)  2.34 us
  transfers between devices with their start and end apart: 6, of which 2 were waited for; matrix products, arithmetic and copies ran while one was open for 0% of the time, Pallas kernels for 0%

commit v1 on v0

v1 whole, which is shorter than its diff:
```python
import functools

import jax
import jax.numpy as jnp
from jax import lax
from jax.experimental import pallas as pl
from jax.experimental.pallas import tpu as pltpu
from jax.sharding import PartitionSpec as P

SWEEPS = 3
BND = 4
clip_level = 0.5
MESH = pl.DeviceIdType.MESH


def swap(v):
    return pltpu.roll(v, v.shape[-1] // 2, v.ndim - 1)


def dup(v):
    return jnp.concatenate([v, v], axis=-1)


def complex_pair(first, second):
    return (
        first[0] * second[0] - first[1] * second[1],
        first[0] * second[1] + first[1] * second[0],
    )


def dot_nt(x, w):
    return lax.dot_general(x, w, (((1,), (1,)), ((), ())), preferred_element_type=jnp.float32)


def kernel(
    n_tm,
    n_region,
    ticks,
    blocks,
    gain_ref,
    target_ref,
    former_ref,
    exc_ref,
    maps_ref,
    att_ref,
    angle_ref,
    flag_ref,
    out_ref,
    rounded,
    halo,
    sent_b,
    got_b,
    cur,
    scan_b,
    pow_re,
    pow_im,
    halo_re,
    halo_im,
    driven,
    driven_sw,
    spin,
    spin_near,
    gains,
    ends,
    ends_near,
    coef,
    halo_send,
    halo_recv,
    spin_send,
    spin_recv,
    gain_send,
    gain_recv,
    end_send,
    end_recv,
    near_send,
    near_recv,
):
    m = lax.axis_index("tm")
    r = lax.axis_index("region")
    right = lax.rem(r + 1, n_region)
    left = lax.rem(r + n_region - 1, n_region)
    sides = (left, right)
    width = out_ref.shape[-1]

    def rows(b):
        return pl.ds(b, ticks, stride=blocks)

    barrier = pltpu.get_barrier_semaphore()
    for k in range(n_tm):
        rank = lax.rem(m + k, n_tm)
        for region in (left, right) if k == 0 else (r, left, right):
            pl.semaphore_signal(
                barrier, inc=1, device_id={"tm": rank, "region": region}, device_id_type=MESH
            )

    lane = lax.broadcasted_iota(jnp.int32, (blocks, width), 1)
    row = lax.broadcasted_iota(jnp.int32, (blocks, width), 0)
    sign = jnp.where(lane < width // 2, -1.0, 1.0)
    upper = row < BND

    for b in range(blocks):
        rounded[b] = former_ref[rows(b), :].astype(jnp.bfloat16)
    modulus = jnp.exp(-dup(att_ref[...]))
    angle = dup(angle_ref[...])
    cosine = modulus * jnp.cos(angle)
    sine = modulus * jnp.sin(angle)
    gain_in = jnp.sqrt((1.0 - cosine) ** 2 + sine**2)
    spin_re = cosine
    spin_im = sign * sine
    spin[0] = spin_re
    spin[1] = spin_im
    total_gain = lax.fori_loop(0, ticks, lambda t, q: q * gain_ref[t], jnp.float32(1.0))
    gains[0] = jnp.full((blocks, width), total_gain, jnp.float32)

    pl.semaphore_wait(barrier, 3 * n_tm - 1)

    def halo_copies(step, src, dst):
        return [
            pltpu.make_async_remote_copy(
                src_ref=src.at[pl.ds(start, BND)],
                dst_ref=dst.at[pl.ds(start, BND)],
                send_sem=halo_send.at[step, side],
                recv_sem=halo_recv.at[step, side],
                device_id={"region": sides[side]},
                device_id_type=MESH,
            )
            for side, start in ((0, 0), (1, blocks - BND))
        ]

    first_halo = halo_copies(0, rounded, halo)
    spin_copies = [
        pltpu.make_async_remote_copy(
            src_ref=spin,
            dst_ref=spin_near.at[side],
            send_sem=spin_send.at[side],
            recv_sem=spin_recv.at[side],
            device_id={"region": sides[side]},
            device_id_type=MESH,
        )
        for side in range(2)
    ]
    gain_copies = [
        pltpu.make_async_remote_copy(
            src_ref=gains.at[0],
            dst_ref=gains.at[k],
            send_sem=gain_send.at[k],
            recv_sem=gain_recv.at[k],
            device_id={"tm": lax.rem(m + k, n_tm)},
            device_id_type=MESH,
        )
        for k in range(1, n_tm)
    ]
    pending = spin_copies + gain_copies
    for copy in first_halo + pending:
        copy.start()

    def partner(b, c):
        return lax.rem(target_ref[b, c], blocks)

    def own_part(b):
        x = jnp.concatenate([rounded[b], rounded[partner(b, 1)]], axis=1)
        return dot_nt(x, jnp.concatenate([maps_ref[b, 0], maps_ref[b, 1]], axis=1))

    def halo_part(b):
        x = jnp.concatenate([halo[partner(b, 2)], halo[partner(b, 3)]], axis=1)
        return dot_nt(x, jnp.concatenate([maps_ref[b, 2], maps_ref[b, 3]], axis=1))

    for b in range(blocks):
        cur[rows(b), :] = own_part(b)

    exc = exc_ref[...].astype(jnp.float32).reshape(ticks, blocks, width)
    exc = exc * gain_in[None]
    driven[...] = exc.reshape(ticks * blocks, width)
    driven_sw[...] = swap(driven[...])

    def powers(base_re, base_im, to_re, to_im):
        def step(t, carry):
            q, re, im = carry
            q = q * gain_ref[t]
            re, im = complex_pair((re, im), (base_re, base_im))
            at = pl.ds(pl.multiple_of(t * blocks, blocks), blocks)
            to_re[at, :] = q * re
            to_im[at, :] = q * im
            return q, re, im

        one = jnp.ones((blocks, width), jnp.float32)
        _, re, im = lax.fori_loop(
            0, ticks, step, (jnp.float32(1.0), one, jnp.zeros_like(one)), unroll=8
        )
        return re, im

    def coefficients(full, base):
        one = (jnp.ones((blocks, width), jnp.float32), jnp.zeros((blocks, width), jnp.float32))
        after, within = one, one
        for j in reversed(range(n_tm)):
            k = lax.rem(m - j + n_tm, n_tm)
            before = j < m
            factor = gains[k]
            end = (factor * full[0], factor * full[1])
            coef[base, k, 0] = after[0]
            coef[base, k, 1] = after[1]
            coef[base, k, 2] = jnp.where(before, within[0], 0.0)
            coef[base, k, 3] = jnp.where(before, within[1], 0.0)
            after = complex_pair(after, end)
            longer = complex_pair(within, end)
            within = tuple(jnp.where(before, a, b) for a, b in zip(longer, within))
        down = (1.0 - after[0], -after[1])
        square = down[0] ** 2 + down[1] ** 2
        head = complex_pair(within, (down[0] / square, -down[1] / square))
        for k in range(n_tm):
            c = complex_pair(head, (coef[base, k, 0], coef[base, k, 1]))
            coef[base, k, 0] = c[0] + coef[base, k, 2]
            coef[base, k, 1] = c[1] + coef[base, k, 3]

    own_full = powers(spin_re, spin_im, pow_re, pow_im)
    for copy in spin_copies + gain_copies:
        copy.wait_recv()
    coefficients(own_full, 0)
    near_re = jnp.where(upper, spin_near[0, 0], spin_near[1, 0])
    near_im = jnp.where(upper, spin_near[0, 1], spin_near[1, 1])
    halo_full = powers(near_re, near_im, halo_re, halo_im)
    coefficients(halo_full, 1)

    limited = dup(flag_ref[...]) == 1

    for copy in first_halo:
        copy.wait_recv()
    for b in range(blocks):
        cur[rows(b), :] += halo_part(b)

    for sweep in range(SWEEPS):

        def scan_step(t, carry):
            s, z = carry
            at = pl.ds(pl.multiple_of(t * blocks, blocks), blocks)
            c = cur[at, :]
            c_sw = swap(c)
            scale = jnp.where(
                limited,
                gain_in * (clip_level * lax.rsqrt(clip_level**2 + (c * c + c_sw * c_sw))),
                gain_in,
            )
            g = gain_ref[t]
            a_re = g * spin_re
            a_im = g * spin_im
            new_s = a_re * s + (a_im * z + (driven[at, :] - scale * c))
            new_z = a_re * z + ((driven_sw[at, :] - scale * c_sw) - a_im * s)
            scan_b[at, :] = new_s
            return new_s, new_z

        zero = jnp.zeros((blocks, width), jnp.float32)
        end_b, _ = lax.fori_loop(0, ticks, scan_step, (zero, zero), unroll=12)
        last = sweep == SWEEPS - 1
        ends[sweep, 0] = end_b
        end_copies = [
            pltpu.make_async_remote_copy(
                src_ref=ends.at[sweep, 0],
                dst_ref=ends.at[sweep, k],
                send_sem=end_send.at[sweep, k],
                recv_sem=end_recv.at[sweep, k],
                device_id={"tm": lax.rem(m + k, n_tm)},
                device_id_type=MESH,
            )
            for k in range(1, n_tm)
        ]
        near_copies = []
        halo_b = []
        if not last:
            near_copies = [
                pltpu.make_async_remote_copy(
                    src_ref=ends.at[sweep, 0],
                    dst_ref=ends_near.at[sweep, side, k],
                    send_sem=near_send.at[sweep, side, k],
                    recv_sem=near_recv.at[sweep, side, k],
                    device_id={"tm": lax.rem(m + k, n_tm), "region": sides[side]},
                    device_id_type=MESH,
                )
                for k in range(n_tm)
                for side in range(2)
            ]
            halo_b = halo_copies(sweep + 1, sent_b.at[sweep], got_b.at[sweep])
        for copy in end_copies + near_copies:
            copy.start()
        if not last:
            for b in range(blocks):
                sent_b[sweep, b] = scan_b[rows(b), :].astype(jnp.bfloat16)
            for copy in halo_b:
                copy.start()
        pending += end_copies + near_copies + halo_b

        def start_state(base, end_of):
            state = jnp.zeros((blocks, width), jnp.float32)
            for k in range(n_tm):
                v = end_of(k)
                state += coef[base, k, 0] * v + coef[base, k, 1] * swap(v)
            return state, swap(state)

        for copy in end_copies:
            copy.wait_recv()
        state, state_sw = start_state(0, lambda k: ends[sweep, k])
        if last:
            shape = (ticks, blocks, width)
            out = (
                pow_re[...].reshape(shape) * state[None]
                + pow_im[...].reshape(shape) * state_sw[None]
                + scan_b[...].reshape(shape)
            )
            out_ref[...] = out.reshape(ticks * blocks, width)
        else:
            if sweep == 0:
                for copy in first_halo:
                    copy.wait_send()
            for b in range(blocks):
                rounded[b] = (
                    pow_re[rows(b), :] * state[b : b + 1]
                    + pow_im[rows(b), :] * state_sw[b : b + 1]
                    + scan_b[rows(b), :]
                ).astype(jnp.bfloat16)
            for b in range(blocks):
                cur[rows(b), :] = own_part(b)
            for copy in near_copies:
                copy.wait_recv()
            state, state_sw = start_state(
                1,
                lambda k: jnp.where(upper, ends_near[sweep, 0, k], ends_near[sweep, 1, k]),
            )
            for copy in halo_b:
                copy.wait_recv()
            for b in range(blocks):
                halo[b] = (
                    halo_re[rows(b), :] * state[b : b + 1]
                    + halo_im[rows(b), :] * state_sw[b : b + 1]
                    + got_b[sweep, b].astype(jnp.float32)
                ).astype(jnp.bfloat16)
            for b in range(blocks):
                cur[rows(b), :] += halo_part(b)
    for copy in pending:
        copy.wait_send()


def local(n_tm, n_region, former, excitation, maps, target, attenuation, angle, flag, gain):
    ticks, blocks, width = former.shape
    flat = (ticks * blocks, width)
    f32, bf16 = jnp.float32, jnp.bfloat16
    rounds = SWEEPS - 1
    vmem = pl.BlockSpec(memory_space=pltpu.VMEM)
    smem = pl.BlockSpec(memory_space=pltpu.SMEM)
    dma = pltpu.SemaphoreType.DMA
    out = pl.pallas_call(
        functools.partial(kernel, n_tm, n_region, ticks, blocks),
        out_shape=jax.ShapeDtypeStruct(flat, f32),
        in_specs=[smem, smem] + [vmem] * 6,
        out_specs=vmem,
        scratch_shapes=[
            pltpu.VMEM((blocks, ticks, width), bf16),
            pltpu.VMEM((blocks, ticks, width), bf16),
            pltpu.VMEM((rounds, blocks, ticks, width), bf16),
            pltpu.VMEM((rounds, blocks, ticks, width), bf16),
            pltpu.VMEM(flat, f32),
            pltpu.VMEM(flat, f32),
            pltpu.VMEM(flat, f32),
            pltpu.VMEM(flat, f32),
            pltpu.VMEM(flat, f32),
            pltpu.VMEM(flat, f32),
            pltpu.VMEM(flat, f32),
            pltpu.VMEM(flat, f32),
            pltpu.VMEM((2, blocks, width), f32),
            pltpu.VMEM((2, 2, blocks, width), f32),
            pltpu.VMEM((n_tm, blocks, width), f32),
            pltpu.VMEM((SWEEPS, n_tm, blocks, width), f32),
            pltpu.VMEM((rounds, 2, n_tm, blocks, width), f32),
            pltpu.VMEM((2, n_tm, 4, blocks, width), f32),
            dma((SWEEPS, 2)),
            dma((SWEEPS, 2)),
            dma((2,)),
            dma((2,)),
            dma((n_tm,)),
            dma((n_tm,)),
            dma((SWEEPS, n_tm)),
            dma((SWEEPS, n_tm)),
            dma((rounds, 2, n_tm)),
            dma((rounds, 2, n_tm)),
        ],
        compiler_params=pltpu.CompilerParams(
            collective_id=0, has_side_effects=True, vmem_limit_bytes=40 * 2**20
        ),
        name="picard",
    )(
        gain,
        target,
        former.reshape(flat),
        excitation.reshape(flat),
        maps,
        attenuation,
        angle,
        flag,
    )
    return out.reshape(ticks, blocks, width)


def solution(mesh):
    in_specs = (
        P(("cases", "tm"), "region", None),
        P(("cases", "tm"), "region", None),
        P("region", None, None, None),
        P("region", None),
        P("region", None),
        P("region", None),
        P(("cases", "region"), None),
        P(("cases", "tm")),
    )
    return jax.shard_map(
        functools.partial(local, mesh.shape["tm"], mesh.shape["region"]),
        mesh=mesh,
        in_specs=in_specs,
        out_specs=P(("cases", "tm"), "region", None),
        check_vma=False,
    )
```

time: 90.4 us -> 30.7 us (0.34)
  blocking collectives: 53.5 us -> 0 us
  Pallas kernels: 0 us -> 25.2 us
  other arithmetic: 11.7 us -> 0 us
  local copies, waits for them, and re-layouts: 12.5 us -> 5.21 us
  starting transfers between devices: 6.07 us -> 0 us
  waiting for transfers between devices: 3.55 us -> 0 us
  matrix products: 1.36 us -> 0 us
  between operations: 1.28 us -> 0.02 us
    all_gather x4 -> x0, blocking collectives: 53.5 us -> none  [the longest x3 39.4 us: local(): lax.all_gather(own_map[1][None], 'tm', axis=0, tiled=True)]
    pallas_call x0 -> x1, Pallas kernels: none -> 25.2 us  [local(): pl.pallas_call(functools.partial(kernel, n_tm, n_region, ticks, blocks),...]
    ppermute x6 -> x0, starting transfers between devices: 6.07 us -> none  [the longest x3 5.45 us: with_halo(): lax.ppermute(lax.slice_in_dim(block, 0, width, axis=dim), axis, backward)]
    sub x45 -> x0, other arithmetic: 4.13 us -> none  [complex_mul(): first_re * second_re - first_im * second_im]
    add x62 -> x0, other arithmetic: 4.07 us -> none  [the longest x33 2.7 us: combine(): complex_mul(late[0], early[1]) + late[1]]
    ppermute x6 -> x0, waiting for transfers between devices: 3.55 us -> none  [the longest x3 3.54 us: with_halo(): lax.ppermute(lax.slice_in_dim(block, block.shape[dim] - width, None, axis...]
    pad x42 -> x0, local copies, waits for them, and re-layouts: 2.43 us -> none  [the longest x34 2.34 us: local(): lax.associative_scan(combine, (incremental_spin, drive), axis=0)]
    gather x3 -> x0, local copies, waits for them, and re-layouts: 1.87 us -> none  [local(): picked = extended[:, local_col, :]]
  transfers between devices with their start and end apart: 6 -> 0, of which waited for: 2 -> 0; matrix products, arithmetic and copies ran while one was open for 0% -> 0% of each run, Pallas kernels for 0% -> 0%
where the time goes in v1:
time: 30.7 us; the launch traced here: 30.4 us
  Pallas kernels  25.2 us (82%)
  local copies, waits for them, and re-layouts  5.21 us (17%)
    pallas_call x1, Pallas kernels, local(): pl.pallas_call(functools.partial(kernel, n_tm, n_region, ticks, blocks),...  25.2 us
    unnamed x16, local copies, waits for them, and re-layouts  5.21 us

profile of v1, /device:TPU:0, one launch (start us, length us, event | category | flops | bytes accessed | tf_op | source)
XLA Modules:
  0.0 30.4 jit_solution(14830022428071470655)
XLA Ops:
  0.0 0.0 copy-start.4
  0.0 0.0 copy-start.3
  0.0 0.0 copy-start.6
  0.0 0.8 %copy.9.target_ref = s32[8,4]{1,0:T(8,128)S(1)} copy(s32[8,4]{0,1:T(4,128)} %param.11) | data formatting | bytes 256 | tf_op args[3]
  0.8 0.0 copy-done.4
  0.8 0.0 copy-done.3
  0.8 0.0 copy-done.6
  0.8 0.0 copy-start
  0.8 1.2 %copy-done = bf16[8,4,128,128]{3,2,1,0:T(8,128)(2,1)S(1)} copy-done((bf16[8,4,128,128]{3,2,1,0:T(8,128)(2,1)S(1)}, bf16[8,4,128,128]{3,2,1,0:T(8,128)(2,1)}, u32[]{:S(2)}) %copy-start) | copy-done | bytes 1048600
  2.0 0.0 copy-start.1
  2.0 0.9 %copy-done.1 = f32[48,8,128]{2,1,0:T(8,128)S(1)} copy-done((f32[48,8,128]{2,1,0:T(8,128)S(1)}, f32[48,8,128]{2,1,0:T(8,128)}, u32[]{:S(2)}) %copy-start.1) | copy-done | bytes 196632
  3.0 0.0 copy-start.2
  3.0 0.9 %copy-done.2 = bf16[48,8,128]{2,1,0:T(8,128)(2,1)S(1)} copy-done((bf16[48,8,128]{2,1,0:T(8,128)(2,1)S(1)}, bf16[48,8,128]{2,1,0:T(8,128)(2,1)}, u32[]{:S(2)}) %copy-start.2) | copy-done | bytes 98328
  3.9 0.0 copy-start.5
  3.9 0.7 %copy-done.5 = s32[8,64]{1,0:T(8,128)S(1)} copy-done((s32[8,64]{1,0:T(8,128)S(1)}, s32[8,64]{1,0:T(8,128)}, u32[]{:S(2)}) %copy-start.5) | copy-done | bytes 2072
  4.5 25.2 %picard.1 = f32[384,128]{1,0:T(8,128)S(1)} custom-call(f32[48]{0:T(128)S(1)} %copy-done.6, s32[8,4]{1,0:T(8,128)S(1)} %copy.9.target_ref, f32[384,128]{1,0:T(8,128)S(1)} %bitcast.4, bf16[384,128]{1,0:T(8,128)(2,1)S(1)} %bitcast.5, bf16[8,4,128,128]{3,2,1,0:T(8,128)(2,1)S(1)} %copy-done, f32[8,64]{1,0:T(8,128)S(1)} %copy-done.3, f32[8,64]{1,0:T(8,128)S(1)} %copy-done.4, ...), custom_call_target="tpu_custom_call" | custom-call | tf_op jit(solution)/shard_map/picard/pallas_call | solution.py:349
  29.8 0.7 %copy.11 = f32[48,8,128]{2,1,0:T(8,128)} copy(f32[48,8,128]{2,1,0:T(8,128)S(1)} %bitcast.3) | data formatting | bytes 393216
Async XLA Ops:
  0.0 0.8 %copy-start.4 = (f32[8,64]{1,0:T(8,128)S(1)}, f32[8,64]{1,0:T(8,128)}, u32[]{:S(2)}) copy-start(f32[8,64]{1,0:T(8,128)} %angle_ref.1) | copy-start | bytes 6148
  0.0 0.8 %copy-start.3 = (f32[8,64]{1,0:T(8,128)S(1)}, f32[8,64]{1,0:T(8,128)}, u32[]{:S(2)}) copy-start(f32[8,64]{1,0:T(8,128)} %att_ref.1) | copy-start | bytes 6148
  0.0 0.8 %copy-start.6 = (f32[48]{0:T(128)S(1)}, f32[48]{0:T(128)}, u32[]{:S(2)}) copy-start(f32[48]{0:T(128)} %gain_ref.1) | copy-start | bytes 580
  0.8 1.2 %copy-start = (bf16[8,4,128,128]{3,2,1,0:T(8,128)(2,1)S(1)}, bf16[8,4,128,128]{3,2,1,0:T(8,128)(2,1)}, u32[]{:S(2)}) copy-start(bf16[8,4,128,128]{3,2,1,0:T(8,128)(2,1)} %maps_ref.1) | copy-start | bytes 3145732
  2.0 0.9 %copy-start.1 = (f32[48,8,128]{2,1,0:T(8,128)S(1)}, f32[48,8,128]{2,1,0:T(8,128)}, u32[]{:S(2)}) copy-start(f32[48,8,128]{2,1,0:T(8,128)} %param.8) | copy-start | bytes 589828
  3.0 0.9 %copy-start.2 = (bf16[48,8,128]{2,1,0:T(8,128)(2,1)S(1)}, bf16[48,8,128]{2,1,0:T(8,128)(2,1)}, u32[]{:S(2)}) copy-start(bf16[48,8,128]{2,1,0:T(8,128)(2,1)} %param.9) | copy-start | bytes 294916
  3.9 0.7 %copy-start.5 = (s32[8,64]{1,0:T(8,128)S(1)}, s32[8,64]{1,0:T(8,128)}, u32[]{:S(2)}) copy-start(s32[8,64]{1,0:T(8,128)} %flag_ref.1) | copy-start | bytes 6148

commit v2 on v1

--- a/solution.py
+++ b/solution.py
@@ -37,6 +37,15 @@
     n_region,
     ticks,
     blocks,
+    gain_hbm,
+    target_hbm,
+    former_hbm,
+    exc_hbm,
+    maps_hbm,
+    att_hbm,
+    angle_hbm,
+    flag_hbm,
+    out_ref,
     gain_ref,
     target_ref,
     former_ref,
@@ -45,7 +54,6 @@
     att_ref,
     angle_ref,
     flag_ref,
-    out_ref,
     rounded,
     halo,
     sent_b,
@@ -58,6 +66,8 @@
     halo_im,
     driven,
     driven_sw,
+    drive,
+    drive_sw,
     spin,
     spin_near,
     gains,
@@ -74,6 +84,7 @@
     end_recv,
     near_send,
     near_recv,
+    fetch_sem,
 ):
     m = lax.axis_index("tm")
     r = lax.axis_index("region")
@@ -85,6 +96,23 @@
     def rows(b):
         return pl.ds(b, ticks, stride=blocks)
 
+    fetches = [
+        pltpu.make_async_copy(src, dst, fetch_sem.at[i])
+        for i, (src, dst) in enumerate(
+            (
+                (former_hbm, former_ref),
+                (att_hbm, att_ref),
+                (angle_hbm, angle_ref),
+                (gain_hbm, gain_ref),
+                (target_hbm, target_ref),
+                (maps_hbm, maps_ref),
+                (exc_hbm, exc_ref),
+                (flag_hbm, flag_ref),
+            )
+        )
+    ]
+    for fetch in fetches:
+        fetch.start()
     barrier = pltpu.get_barrier_semaphore()
     for k in range(n_tm):
         rank = lax.rem(m + k, n_tm)
@@ -98,8 +126,11 @@
     sign = jnp.where(lane < width // 2, -1.0, 1.0)
     upper = row < BND
 
+    fetches[0].wait()
     for b in range(blocks):
         rounded[b] = former_ref[rows(b), :].astype(jnp.bfloat16)
+    for fetch in fetches[1:4]:
+        fetch.wait()
     modulus = jnp.exp(-dup(att_ref[...]))
     angle = dup(angle_ref[...])
     cosine = modulus * jnp.cos(angle)
@@ -112,6 +143,67 @@
     total_gain = lax.fori_loop(0, ticks, lambda t, q: q * gain_ref[t], jnp.float32(1.0))
     gains[0] = jnp.full((blocks, width), total_gain, jnp.float32)
 
+    def partner(b, c):
+        return lax.rem(target_ref[c, b], blocks)
+
+    def own_part(b):
+        x = jnp.concatenate([rounded[b], rounded[partner(b, 1)]], axis=1)
+        return dot_nt(x, jnp.concatenate([maps_ref[b, 0], maps_ref[b, 1]], axis=1))
+
+    def halo_part(b):
+        x = jnp.concatenate([halo[partner(b, 2)], halo[partner(b, 3)]], axis=1)
+        return dot_nt(x, jnp.concatenate([maps_ref[b, 2], maps_ref[b, 3]], axis=1))
+
+    for fetch in fetches[4:]:
+        fetch.wait()
+    for b in range(blocks):
+        cur[rows(b), :] = own_part(b)
+
+    exc = exc_ref[...].astype(jnp.float32).reshape(ticks, blocks, width)
+    exc = exc * gain_in[None]
+    driven[...] = exc.reshape(ticks * blocks, width)
+    driven_sw[...] = swap(driven[...])
+
+    def powers(base_re, base_im, to_re, to_im):
+        def step(t, carry):
+            q, re, im = carry
+            q = q * gain_ref[t]
+            re, im = complex_pair((re, im), (base_re, base_im))
+            at = pl.ds(pl.multiple_of(t * blocks, blocks), blocks)
+            to_re[at, :] = q * re
+            to_im[at, :] = q * im
+            return q, re, im
+
+        one = jnp.ones((blocks, width), jnp.float32)
+        _, re, im = lax.fori_loop(
+            0, ticks, step, (jnp.float32(1.0), one, jnp.zeros_like(one)), unroll=True
+        )
+        return re, im
+
+    def coefficients(full, base):
+        one = (jnp.ones((blocks, width), jnp.float32), jnp.zeros((blocks, width), jnp.float32))
+        after, within = one, one
+        for j in reversed(range(n_tm)):
+            k = lax.rem(m - j + n_tm, n_tm)
+            before = j < m
+            factor = gains[k]
+            end = (factor * full[0], factor * full[1])
+            coef[base, k, 0] = after[0]
+            coef[base, k, 1] = after[1]
+            coef[base, k, 2] = jnp.where(before, within[0], 0.0)
+            coef[base, k, 3] = jnp.where(before, within[1], 0.0)
+            after = complex_pair(after, end)
+            longer = complex_pair(within, end)
+            within = tuple(jnp.where(before, a, b) for a, b in zip(longer, within))
+        down = (1.0 - after[0], -after[1])
+        square = down[0] ** 2 + down[1] ** 2
+        head = complex_pair(within, (down[0] / square, -down[1] / square))
+        for k in range(n_tm):
+            c = complex_pair(head, (coef[base, k, 0], coef[base, k, 1]))
+            coef[base, k, 0] = c[0] + coef[base, k, 2]
+            coef[base, k, 1] = c[1] + coef[base, k, 3]
+
+    own_full = powers(spin_re, spin_im, pow_re, pow_im)
     pl.semaphore_wait(barrier, 3 * n_tm - 1)
 
     def halo_copies(step, src, dst):
@@ -154,65 +246,6 @@
     for copy in first_halo + pending:
         copy.start()
 
-    def partner(b, c):
-        return lax.rem(target_ref[b, c], blocks)
-
-    def own_part(b):
-        x = jnp.concatenate([rounded[b], rounded[partner(b, 1)]], axis=1)
-        return dot_nt(x, jnp.concatenate([maps_ref[b, 0], maps_ref[b, 1]], axis=1))
-
-    def halo_part(b):
-        x = jnp.concatenate([halo[partner(b, 2)], halo[partner(b, 3)]], axis=1)
-        return dot_nt(x, jnp.concatenate([maps_ref[b, 2], maps_ref[b, 3]], axis=1))
-
-    for b in range(blocks):
-        cur[rows(b), :] = own_part(b)
-
-    exc = exc_ref[...].astype(jnp.float32).reshape(ticks, blocks, width)
-    exc = exc * gain_in[None]
-    driven[...] = exc.reshape(ticks * blocks, width)
-    driven_sw[...] = swap(driven[...])
-
-    def powers(base_re, base_im, to_re, to_im):
-        def step(t, carry):
-            q, re, im = carry
-            q = q * gain_ref[t]
-            re, im = complex_pair((re, im), (base_re, base_im))
-            at = pl.ds(pl.multiple_of(t * blocks, blocks), blocks)
-            to_re[at, :] = q * re
-            to_im[at, :] = q * im
-            return q, re, im
-
-        one = jnp.ones((blocks, width), jnp.float32)
-        _, re, im = lax.fori_loop(
-            0, ticks, step, (jnp.float32(1.0), one, jnp.zeros_like(one)), unroll=8
-        )
-        return re, im
-
-    def coefficients(full, base):
-        one = (jnp.ones((blocks, width), jnp.float32), jnp.zeros((blocks, width), jnp.float32))
-        after, within = one, one
-        for j in reversed(range(n_tm)):
-            k = lax.rem(m - j + n_tm, n_tm)
-            before = j < m
-            factor = gains[k]
-            end = (factor * full[0], factor * full[1])
-            coef[base, k, 0] = after[0]
-            coef[base, k, 1] = after[1]
-            coef[base, k, 2] = jnp.where(before, within[0], 0.0)
-            coef[base, k, 3] = jnp.where(before, within[1], 0.0)
-            after = complex_pair(after, end)
-            longer = complex_pair(within, end)
-            within = tuple(jnp.where(before, a, b) for a, b in zip(longer, within))
-        down = (1.0 - after[0], -after[1])
-        square = down[0] ** 2 + down[1] ** 2
-        head = complex_pair(within, (down[0] / square, -down[1] / square))
-        for k in range(n_tm):
-            c = complex_pair(head, (coef[base, k, 0], coef[base, k, 1]))
-            coef[base, k, 0] = c[0] + coef[base, k, 2]
-            coef[base, k, 1] = c[1] + coef[base, k, 3]
-
-    own_full = powers(spin_re, spin_im, pow_re, pow_im)
     for copy in spin_copies + gain_copies:
         copy.wait_recv()
     coefficients(own_full, 0)
@@ -230,26 +263,32 @@
 
     for sweep in range(SWEEPS):
 
+        c = cur[...]
+        c_sw = swap(c)
+        c = c.reshape(ticks, blocks, width)
+        c_sw = c_sw.reshape(ticks, blocks, width)
+        cut = gain_in * clip_level
+        scale = jnp.where(
+            limited[None],
+            cut[None] * lax.rsqrt(clip_level**2 + (c * c + c_sw * c_sw)),
+            gain_in[None],
+        )
+        drive[...] = driven[...] - (scale * c).reshape(ticks * blocks, width)
+        drive_sw[...] = driven_sw[...] - (scale * c_sw).reshape(ticks * blocks, width)
+
         def scan_step(t, carry):
             s, z = carry
             at = pl.ds(pl.multiple_of(t * blocks, blocks), blocks)
-            c = cur[at, :]
-            c_sw = swap(c)
-            scale = jnp.where(
-                limited,
-                gain_in * (clip_level * lax.rsqrt(clip_level**2 + (c * c + c_sw * c_sw))),
-                gain_in,
-            )
             g = gain_ref[t]
             a_re = g * spin_re
             a_im = g * spin_im
-            new_s = a_re * s + (a_im * z + (driven[at, :] - scale * c))
-            new_z = a_re * z + ((driven_sw[at, :] - scale * c_sw) - a_im * s)
+            new_s = a_re * s + (a_im * z + (drive[at, :]))
+            new_z = a_re * z + (drive_sw[at, :] - a_im * s)
             scan_b[at, :] = new_s
             return new_s, new_z
 
         zero = jnp.zeros((blocks, width), jnp.float32)
-        end_b, _ = lax.fori_loop(0, ticks, scan_step, (zero, zero), unroll=12)
+        end_b, _ = lax.fori_loop(0, ticks, scan_step, (zero, zero), unroll=True)
         last = sweep == SWEEPS - 1
         ends[sweep, 0] = end_b
         end_copies = [
@@ -344,18 +383,28 @@
     f32, bf16 = jnp.float32, jnp.bfloat16
     rounds = SWEEPS - 1
     vmem = pl.BlockSpec(memory_space=pltpu.VMEM)
-    smem = pl.BlockSpec(memory_space=pltpu.SMEM)
+    hbm = pl.BlockSpec(memory_space=pl.ANY)
     dma = pltpu.SemaphoreType.DMA
     out = pl.pallas_call(
         functools.partial(kernel, n_tm, n_region, ticks, blocks),
         out_shape=jax.ShapeDtypeStruct(flat, f32),
-        in_specs=[smem, smem] + [vmem] * 6,
+        in_specs=[hbm] * 8,
         out_specs=vmem,
         scratch_shapes=[
+            pltpu.SMEM(gain.shape, f32),
+            pltpu.SMEM(target.shape[::-1], target.dtype),
+            pltpu.VMEM(flat, f32),
+            pltpu.VMEM(flat, bf16),
+            pltpu.VMEM(maps.shape, bf16),
+            pltpu.VMEM(attenuation.shape, f32),
+            pltpu.VMEM(angle.shape, f32),
+            pltpu.VMEM(flag.shape, flag.dtype),
             pltpu.VMEM((blocks, ticks, width), bf16),
             pltpu.VMEM((blocks, ticks, width), bf16),
             pltpu.VMEM((rounds, blocks, ticks, width), bf16),
             pltpu.VMEM((rounds, blocks, ticks, width), bf16),
+            pltpu.VMEM(flat, f32),
+            pltpu.VMEM(flat, f32),
             pltpu.VMEM(flat, f32),
             pltpu.VMEM(flat, f32),
             pltpu.VMEM(flat, f32),
@@ -380,14 +429,15 @@
             dma((SWEEPS, n_tm)),
             dma((rounds, 2, n_tm)),
             dma((rounds, 2, n_tm)),
+            dma((8,)),
         ],
         compiler_params=pltpu.CompilerParams(
-            collective_id=0, has_side_effects=True, vmem_limit_bytes=40 * 2**20
+            collective_id=0, has_side_effects=True
         ),
         name="picard",
     )(
         gain,
-        target,
+        target.T,
         former.reshape(flat),
         excitation.reshape(flat),
         maps,

time: 30.7 us -> 26.3 us (0.86)
  local copies, waits for them, and re-layouts: 5.21 us -> 1.62 us
  Pallas kernels: 25.2 us -> 24.5 us
    unnamed x16 -> x1, local copies, waits for them, and re-layouts: 5.21 us -> 1.62 us
    pallas_call x1, Pallas kernels: 25.2 us -> 24.5 us  [local(): pl.pallas_call(functools.partial(kernel, n_tm, n_region, ticks, blocks),...]
where the time goes in v2:
time: 26.3 us; the launch traced here: 26.1 us
  Pallas kernels  24.5 us (93%)
  local copies, waits for them, and re-layouts  1.62 us (6%)
    pallas_call x1, Pallas kernels, local(): pl.pallas_call(functools.partial(kernel, n_tm, n_region, ticks, blocks),...  24.5 us
    unnamed x1, local copies, waits for them, and re-layouts  1.62 us

profile of v2, /device:TPU:0, one launch (start us, length us, event | category | flops | bytes accessed | tf_op | source)
XLA Modules:
  0.0 26.1 jit_solution(8597693887030334801)
XLA Ops:
  0.0 24.5 %picard.1 = f32[384,128]{1,0:T(8,128)} custom-call(f32[48]{0:T(128)} %gain_hbm.1, s32[4,8]{1,0:T(4,128)} %bitcast.7, f32[384,128]{1,0:T(8,128)} %bitcast.5, bf16[384,128]{1,0:T(8,128)(2,1)} %bitcast.6, bf16[8,4,128,128]{3,2,1,0:T(8,128)(2,1)} %maps_hbm.1, f32[8,64]{1,0:T(8,128)} %att_hbm.1, f32[8,64]{1,0:T(8,128)} %angle_hbm.1, s32[8,64]{1,0:T(8,128)} %flag_hbm.1), custom_call_target="tpu_custom_call" | custom-call | tf_op jit(solution)/shard_map/picard/pallas_call | solution.py:388
  24.5 1.6 %copy.10 = f32[48,8,128]{2,1,0:T(8,128)} copy(f32[48,8,128]{2,1,0:T(8,128)} %bitcast.4) | data formatting | bytes 393216

commit v3 on v2

--- a/solution.py
+++ b/solution.py
@@ -246,14 +246,6 @@
     for copy in first_halo + pending:
         copy.start()
 
-    for copy in spin_copies + gain_copies:
-        copy.wait_recv()
-    coefficients(own_full, 0)
-    near_re = jnp.where(upper, spin_near[0, 0], spin_near[1, 0])
-    near_im = jnp.where(upper, spin_near[0, 1], spin_near[1, 1])
-    halo_full = powers(near_re, near_im, halo_re, halo_im)
-    coefficients(halo_full, 1)
-
     limited = dup(flag_ref[...]) == 1
 
     for copy in first_halo:
@@ -326,6 +318,15 @@
             for copy in halo_b:
                 copy.start()
         pending += end_copies + near_copies + halo_b
+
+        if sweep == 0:
+            for copy in spin_copies + gain_copies:
+                copy.wait_recv()
+            coefficients(own_full, 0)
+            near_re = jnp.where(upper, spin_near[0, 0], spin_near[1, 0])
+            near_im = jnp.where(upper, spin_near[0, 1], spin_near[1, 1])
+            halo_full = powers(near_re, near_im, halo_re, halo_im)
+            coefficients(halo_full, 1)
 
         def start_state(base, end_of):
             state = jnp.zeros((blocks, width), jnp.float32)

time: 26.3 us -> 24.9 us (0.947)
  Pallas kernels: 24.5 us -> 23.1 us
    pallas_call x1, Pallas kernels: 24.5 us -> 23.1 us  [local(): pl.pallas_call(functools.partial(kernel, n_tm, n_region, ticks, blocks),...]
where the time goes in v3:
time: 24.9 us; the launch traced here: 24.7 us
  Pallas kernels  23.1 us (93%)
  local copies, waits for them, and re-layouts  1.62 us (7%)
    pallas_call x1, Pallas kernels, local(): pl.pallas_call(functools.partial(kernel, n_tm, n_region, ticks, blocks),...  23.1 us
    unnamed x1, local copies, waits for them, and re-layouts  1.62 us

profile of v3, /device:TPU:0, one launch (start us, length us, event | category | flops | bytes accessed | tf_op | source)
XLA Modules:
  0.0 24.7 jit_solution(1839935457822558155)
XLA Ops:
  0.0 23.1 %picard.1 = f32[384,128]{1,0:T(8,128)} custom-call(f32[48]{0:T(128)} %gain_hbm.1, s32[4,8]{1,0:T(4,128)} %bitcast.7, f32[384,128]{1,0:T(8,128)} %bitcast.5, bf16[384,128]{1,0:T(8,128)(2,1)} %bitcast.6, bf16[8,4,128,128]{3,2,1,0:T(8,128)(2,1)} %maps_hbm.1, f32[8,64]{1,0:T(8,128)} %att_hbm.1, f32[8,64]{1,0:T(8,128)} %angle_hbm.1, s32[8,64]{1,0:T(8,128)} %flag_hbm.1), custom_call_target="tpu_custom_call" | custom-call | tf_op jit(solution)/shard_map/picard/pallas_call | solution.py:389
  23.1 1.6 %copy.10 = f32[48,8,128]{2,1,0:T(8,128)} copy(f32[48,8,128]{2,1,0:T(8,128)} %bitcast.4) | data formatting | bytes 393216
